TPU v7x, 32 devices: a whole 2x2x4 slice. The times are simulated.
32 devices in a mesh: grp: 2 (over x), tp: 16 (over z, y, core).
Axes of the slice: x: 2, y: 2, z: 4, core: 2. Of those that a mesh axis runs over, the one named last changes fastest.
Arguments:
- queries: bfloat16 [4, 128, 8192], P('grp', None, 'tp'), parts along dimension 0, may hold values from -72 to 72
- kv_cache: bfloat16 [2, 4, 2048, 512], P(None, 'grp'), parts along dimension 1, may hold values from -3 to 3
- span_kv: bfloat16 [2, 4, 128, 512], P(None, 'grp'), parts along dimension 1, may hold values from -4 to 4
- prefix_len: int32 [4], P('grp'), parts along dimension 0, may hold values from 512 to 2048, as said below
- residual: bfloat16 [512, 16384], P(('grp', 'tp')), parts along dimension 0, may hold values from -1.1953125 to 1.1953125
- out_weight: bfloat16 [8192, 16384], P('tp'), may hold values from -0.0625 to 0.0625
- sign_bits: int32 [16384], replicated, may hold values from 0 to 1
Outputs:
- stream: bfloat16 [512, 16384], P(('grp', 'tp')), parts along dimension 0
- normed: bfloat16 [512, 16384], P('grp'), parts along dimension 0
There are 2 independent parts, one for each index of `grp`. A program takes and returns all parts, laid end to end along the dimension named above; an argument that names none is the same for every part. Nothing has to cross between parts.
Inputs may be any that keep to these rules, and one draw needn't show every extreme that they name: `prefix_len`: some sequence has all 2048 positions in use in every draw.
All inputs are finite; a program needn't handle non-finite values.
Results may differ from a plain program's by a relative error of at most 0.0064.
Values may be sent and summed in bfloat16 or wider, within the bound.
A program may use at most 192 MiB of HBM per device.

v0:
```python
import math

import jax
import jax.numpy as jnp
from jax import lax
from jax.sharding import PartitionSpec as P

H = 64
KVH = 4
HD = 128
HB = 256


def hadamard(size):
    indices = jnp.arange(size, dtype=jnp.int32)
    common = indices[:, None] & indices[None, :]
    parity = jnp.zeros((size, size), jnp.int32)
    for position in range(size.bit_length() - 1):
        parity = parity + (common >> position & 1)
    return (1 - 2 * (parity % 2)).astype(jnp.float32) / math.sqrt(size)


def rotate_rows(values, sign_values, hadamard_table):
    rows_here, columns = values.shape
    block_len = hadamard_table.shape[0]
    rotated = (values * sign_values).reshape(rows_here, columns // block_len, block_len)
    rotated = jnp.einsum("rkb,bc->rkc", rotated, hadamard_table, precision=lax.Precision.HIGHEST)
    return rotated.reshape(rows_here, columns)


def attention(queries, keys_all, values_all, prefix_len):
    seq_count, span_len, local_cols = queries.shape
    heads_here = local_cols // HD
    prefix_cap = keys_all.shape[1] - span_len
    query_heads = queries.reshape(seq_count, span_len, heads_here, HD)
    scores = jnp.einsum(
        "bthd,bjd->bhtj", query_heads, keys_all, preferred_element_type=jnp.float32
    ) / math.sqrt(HD)
    positions = jnp.arange(prefix_cap + span_len, dtype=jnp.int32)
    query_pos = jnp.arange(span_len, dtype=jnp.int32)
    visible = jnp.where(
        positions[None, None, :] < prefix_cap,
        positions[None, None, :] < prefix_len[:, None, None],
        positions[None, None, :] - prefix_cap <= query_pos[None, :, None],
    )
    visible = visible[:, None]
    scores = jnp.where(visible, scores, -1e30)
    largest = jnp.max(scores, axis=-1, keepdims=True)
    powered = jnp.where(visible, jnp.exp(scores - largest), 0.0)
    weights = (powered / jnp.sum(powered, axis=-1, keepdims=True)).astype(jnp.bfloat16)
    combined = jnp.einsum("bhtj,bjd->bthd", weights, values_all, preferred_element_type=jnp.float32)
    return combined.astype(jnp.bfloat16).reshape(seq_count * span_len, heads_here * HD)


def body(queries, kv_cache, span_kv, prefix_len, residual, out_weight, sign_bits):
    tp_index = lax.axis_index("tp")
    heads_here = queries.shape[2] // HD
    kv_head = tp_index * heads_here // (H // KVH)
    cache_head = lax.dynamic_slice_in_dim(kv_cache, kv_head * HD, HD, 3)
    span_head = lax.dynamic_slice_in_dim(span_kv, kv_head * HD, HD, 3)
    keys_all = jnp.concatenate([cache_head[0], span_head[0]], axis=1)
    values_all = jnp.concatenate([cache_head[1], span_head[1]], axis=1)
    attended = attention(queries, keys_all, values_all, prefix_len)
    hadamard_table = hadamard(HB)
    sign_values = (2 * sign_bits - 1).astype(jnp.float32)
    partial_value = jnp.dot(attended, out_weight, preferred_element_type=jnp.float32).astype(
        jnp.bfloat16
    )
    arrived = lax.all_to_all(partial_value[None], "tp", split_axis=1, concat_axis=0, tiled=True)
    reduced = jnp.sum(arrived.astype(jnp.float32), axis=0)
    rotated = rotate_rows(reduced, sign_values, hadamard_table)
    stream = (residual.astype(jnp.float32) + rotated).astype(jnp.bfloat16)
    stream_wide = lax.optimization_barrier(stream).astype(jnp.float32)
    normed = (
        stream_wide * lax.rsqrt(jnp.mean(stream_wide * stream_wide, axis=-1, keepdims=True) + 1e-05)
    ).astype(jnp.bfloat16)
    gathered = lax.all_gather(normed, "tp", axis=0, tiled=True)
    return (stream, gathered)


def solution(mesh):
    in_specs = (
        P("grp", None, "tp"),
        P(None, "grp", None, None),
        P(None, "grp", None, None),
        P("grp"),
        P(("grp", "tp"), None),
        P("tp", None),
        P(),
    )
    out_specs = (P(("grp", "tp"), None), P("grp", None))
    return jax.shard_map(body, mesh=mesh, in_specs=in_specs, out_specs=out_specs, check_vma=False)
```

profile of v0, /device:TPU:0, one launch (start us, length us, event | category | flops | bytes accessed | tf_op | source)
XLA Modules:
  0.0 456.4 jit_solution(1352957438881092575)
XLA Ops:
  7.2 0.0 copy-start
  7.2 1.7 dynamic-slice_bitcast_fusion.1
  9.0 0.9 dynamic-slice_bitcast_fusion.3
  9.9 1.0 iota_compare_fusion
  10.9 0.7 iota_compare_fusion.1
  11.7 1.9 broadcast_select_fusion
  13.6 5.9 %fusion.59 = (f32[2,4,128]{2,1,0:T(4,128)S(1)}, f32[2,4,128,2176]{2,3,1,0:T(8,128)}) fusion(pred[2,128,2176]{1,2,0:T(8,128)(4,1)S(1)} %broadcast_select_fusion, bf16[2,128,128]{2,1,0:T(8,128)(2,1)S(1)} %get-tuple-element.5, bf16[2,2048,128]{2,1,0:T(8,128)(2,1)S(1)} %get-tuple-element.3, bf16[2,128,512]{2,1,0:T(8,128)(2,1)S(1)} %copy-done), kind=kOutput, calls=%fused_computation.78 | convolution fusion | flops 583796864 | bytes 10850304 | tf_op jit(solution)/shard_map/sub | solution.py:49
  19.5 4.4 fusion.10
  23.9 0.2 copy.19
  24.1 10.5 %fusion.1 = bf16[1,256,16384]{2,1,0:T(8,128)(2,1)S(1)} fusion(bf16[512,16384]{1,0:T(8,128)(2,1)} %param.12, bf16[32,8,4,128]{3,2,1,0:T(4,128)(2,1)S(1)} %bitcast.73), kind=kOutput, calls=%fused_computation.2 | convolution fusion | flops 4299161600 | bytes 25427968 | tf_op jit(solution)/shard_map/dot_general | solution.py:66
  34.7 30.9 %copy.47 = bf16[1,256,16384]{2,0,1:T(2,128)(2,1)} copy(bf16[1,256,16384]{2,1,0:T(8,128)(2,1)S(1)} %fusion.1) | data formatting | bytes 16777216 | tf_op jit(solution)/shard_map/broadcast_in_dim | solution.py:69
  65.6 0.5 broadcast.117
  66.1 51.2 %reduce = bf16[256,16384]{1,0:T(8,128)(2,1)} reduce(bf16[256,1,16384]{2,1,0:T(2,128)(2,1)} %bitcast.69, bf16[]{:T(256)} %broadcast.117), dimensions={1}, to_apply=%bitcast.67.reduce_sub_computation | reduce | bytes 16777218
  117.3 14.5 %reshape.99 = bf16[16,2,131072]{2,1,0:T(2,128)(2,1)} reshape(bf16[256,16384]{1,0:T(8,128)(2,1)} %reduce) | data formatting | bytes 16777216
  131.8 7.6 %all-to-all-start = ((bf16[16,2,131072]{2,1,0:T(2,128)(2,1)}), bf16[16,2,131072]{2,1,0:T(2,128)(2,1)}, u32[]{:S(2)}, u32[]{:S(2)}) async-start(bf16[16,2,131072]{2,1,0:T(2,128)(2,1)} %reshape.99), calls=%async_computation | async-start | bytes 16777216 | tf_op jit(solution)/shard_map/all_to_all | solution.py:69
  139.3 0.2 all-gather.2.cloned.1.call-start
  139.6 150.4 %all-to-all-done = bf16[16,2,131072]{2,1,0:T(2,128)(2,1)} async-done(((bf16[16,2,131072]{2,1,0:T(2,128)(2,1)}), bf16[16,2,131072]{2,1,0:T(2,128)(2,1)}, u32[]{:S(2)}, u32[]{:S(2)}) %all-to-all-start) | async-done | bytes 8388640 | tf_op jit(solution)/shard_map/all_to_all | solution.py:69
  290.1 16.4 %reshape.100 = bf16[256,1,16384]{2,1,0:T(2,128)(2,1)} reshape(bf16[16,2,131072]{2,1,0:T(2,128)(2,1)} %all-to-all-done) | data formatting | bytes 16777216
  306.4 18.3 %copy.26 = f32[1,256,16384]{2,1,0:T(8,128)} copy(bf16[1,256,16384]{2,0,1:T(2,128)(2,1)} %bitcast.70) | data formatting | bytes 25165824
  324.7 6.6 %reduce_sum.30 = f32[16,16384]{1,0:T(8,128)S(1)} reduce(f32[16,16,16384]{2,1,0:T(8,128)} %bitcast.68, f32[]{:T(128)} %constant.66.clone.1), dimensions={0}, to_apply=%region_2.3 | reduce | flops 3932160 | bytes 17825796 | tf_op jit(solution)/shard_map/reduce_sum | solution.py:70
  331.3 0.0 copy-start.3
  331.3 0.3 copy.29
  331.6 0.1 bitcast_multiply_fusion
  331.8 1.3 fusion.22
  333.1 0.6 copy.30
  333.7 0.1 add_convert_fusion
  333.8 0.0 copy-start.2
  333.8 0.2 fusion.13
  334.1 1.0 fusion.14
  335.1 0.0 all-gather.2.cloned.1.call-update
  335.1 106.8 %all-gather.2.cloned.1.call-done = bf16[256,16384]{1,0:T(8,128)(2,1)} async-done(((bf16[16,16384]{1,0:T(8,128)(2,1)}), bf16[256,16384]{1,0:T(8,128)(2,1)}) %all-gather.2.cloned.1.call-update) | async-done | bytes 8388624 | tf_op jit(solution)/shard_map/all_gather | solution.py:77
  441.9 7.7 %copy.49 = bf16[256,16384]{1,0:T(8,128)(2,1)} copy(bf16[256,16384]{1,0:T(8,128)(2,1)} %all-gather.2.cloned.1.call-done) | data formatting | bytes 16777216
  (12 shorter events, 0.1 us)
Async XLA Ops:
  7.2 6.4 %copy-start = (bf16[2,128,512]{2,1,0:T(8,128)(2,1)S(1)}, bf16[2,128,512]{2,1,0:T(8,128)(2,1)}, u32[]{:S(2)}) copy-start(bf16[2,128,512]{2,1,0:T(8,128)(2,1)} %param.7) | copy-start | bytes 786436
  131.8 7.8 %copy-start.4 = (s32[16384]{0:T(1024)S(1)}, s32[16384]{0:T(1024)}, u32[]{:S(2)}) copy-start(s32[16384]{0:T(1024)} %param.13) | copy-start | bytes 196612
  131.8 158.3 %all-to-all-start = ((bf16[16,2,131072]{2,1,0:T(2,128)(2,1)}), bf16[16,2,131072]{2,1,0:T(2,128)(2,1)}, u32[]{:S(2)}, u32[]{:S(2)}) async-start(bf16[16,2,131072]{2,1,0:T(2,128)(2,1)} %reshape.99), calls=%async_computation | async-start | bytes 16777216 | tf_op jit(solution)/shard_map/all_to_all | solution.py:69
  139.3 302.6 %all-gather.2.cloned.1.call-start = ((), (), s32[]{:S(2)}) async-start(), calls=%async_computation.1 | async-start | bytes 8912896 | tf_op jit(solution)/shard_map/all_gather | solution.py:77
  331.3 2.4 copy-start.3
  333.8 115.8 %copy-start.2 = (bf16[16,16384]{1,0:T(8,128)(2,1)}, bf16[16,16384]{1,0:T(8,128)(2,1)S(1)}, u32[]{:S(2)}) copy-start(bf16[16,16384]{1,0:T(8,128)(2,1)S(1)} %add_convert_fusion) | copy-start | bytes 1572868
  335.1 114.5 %copy-start.1 = (bf16[2,128,512]{2,1,0:T(8,128)(2,1)S(1)}, bf16[2,128,512]{2,1,0:T(8,128)(2,1)}, u32[]{:S(2)}) copy-start(bf16[2,128,512]{2,1,0:T(8,128)(2,1)} %param.7) | copy-start | bytes 786436
Sparse Core Ops, SparseCore 0:
  335.2 106.6 all-gather.1
where the time goes:
time: 458 us; the launch traced here: 456 us
  waiting for transfers between devices  257 us (56%)
  local copies, waits for them, and re-layouts  92 us (20%)
  other arithmetic  62.9 us (14%)
  matrix products  22.2 us (5%)
  between operations  14.2 us (3%)
  starting transfers between devices  7.8 us (2%)
    all_to_all x1, waiting for transfers between devices, body(): lax.all_to_all(partial_value[None], 'tp', split_axis=1, concat_axis=0, ti...  150 us
    all_gather x1, waiting for transfers between devices, body(): gathered = lax.all_gather(normed, 'tp', axis=0, tiled=True)  107 us
    unnamed x17, local copies, waits for them, and re-layouts  58.2 us
    unnamed x1, other arithmetic  51.2 us
    broadcast_in_dim x1, local copies, waits for them, and re-layouts, body(): partial_value[None]  30.9 us
    dot_general x1, matrix products, body(): jnp.dot(attended, out_weight, preferred_element_type=jnp.float32)  10.5 us
  transfers between devices with their start and end apart: 2, of which 2 were waited for; matrix products, arithmetic and copies ran while one was open for 0% of the time, Pallas kernels for 0%

commit v1 on v0

v1 whole, which is shorter than its diff:
```python
import functools
import math

import jax
import jax.numpy as jnp
from jax import lax
from jax.experimental import pallas as pl
from jax.experimental.pallas import tpu as pltpu
from jax.sharding import PartitionSpec as P

H = 64
KVH = 4
HD = 128
HB = 256
CHUNK = 1024
MIB = 1 << 20


def hadamard(size):
    indices = jnp.arange(size, dtype=jnp.int32)
    common = indices[:, None] & indices[None, :]
    parity = jnp.zeros((size, size), jnp.int32)
    for position in range(size.bit_length() - 1):
        parity = parity + (common >> position & 1)
    return (1 - 2 * (parity % 2)).astype(jnp.float32) / math.sqrt(size)


def attention_kernel(scalars, q_ref, cache_ref, span_ref, out_ref):
    seq = pl.program_id(0)
    length = scalars[1 + seq]
    prefix_cap = cache_ref.shape[2]
    span = span_ref.shape[2]
    _, _, z_here, rows, local_cols = out_ref.shape
    scale = math.log2(math.e) / math.sqrt(HD)
    keys, values = cache_ref[0, 0], cache_ref[1, 0]
    span_keys, span_values = span_ref[0, 0], span_ref[1, 0]
    trans = (((1,), (1,)), ((), ()))
    shown = lax.broadcasted_iota(jnp.int32, (span, prefix_cap), 1) < length
    token = lax.broadcasted_iota(jnp.int32, (span, span), 0)
    causal = lax.broadcasted_iota(jnp.int32, (span, span), 1) <= token
    for head in range(local_cols // HD):
        at = slice(head * HD, (head + 1) * HD)
        q = q_ref[0, :, at]
        s0 = lax.dot_general(q, keys, trans, preferred_element_type=jnp.float32)
        s1 = lax.dot_general(q, span_keys, trans, preferred_element_type=jnp.float32)
        s0 = jnp.where(shown, s0, -1e30)
        s1 = jnp.where(causal, s1, -1e30)
        top = jnp.maximum(jnp.max(s0, axis=1, keepdims=True), jnp.max(s1, axis=1, keepdims=True))
        p0 = jnp.exp2((s0 - top) * scale)
        p1 = jnp.exp2((s1 - top) * scale)
        total = jnp.sum(p0, axis=1, keepdims=True) + jnp.sum(p1, axis=1, keepdims=True)
        mixed = jnp.dot(p0.astype(jnp.bfloat16), values, preferred_element_type=jnp.float32)
        mixed += jnp.dot(p1.astype(jnp.bfloat16), span_values, preferred_element_type=jnp.float32)
        mixed = (mixed / total).astype(jnp.bfloat16)
        for z in range(z_here):
            for y in range(2):
                for core in range(2):
                    first = ((z * 2 + y) * 2 + core) * rows
                    out_ref[core, y, z, :, at] = mixed[first : first + rows]


def exchange_kernel(
    att_ref, w_ref, res_ref, sign_ref, had_ref, g_ref,
    wbuf, part, got_a, got_b, got_c, own,
    w_sem, own_sem, a_send, a_recv, b_send, b_recv, c_send, c_recv,
    z_send, z_recv, y_send, y_recv, d_send, d_recv,
):
    chunks, z_count, rows, cols = got_b.shape
    me = lax.axis_index("tp")
    core = lax.rem(me, 2)
    y = lax.rem(me // 2, 2)
    z = me // 4
    core_peer = me + 1 - 2 * core
    y_peer = me + 2 - 4 * y

    def z_other(step):
        return lax.rem(z + step, z_count)

    def z_peer(step):
        return z_other(step) * 4 + y * 2 + core

    def at(k):
        return pl.ds(pl.multiple_of(k * cols, cols), cols)

    def remote(src, dst, send, recv, peer):
        return pltpu.make_async_remote_copy(
            src_ref=src, dst_ref=dst, send_sem=send, recv_sem=recv,
            device_id={"tp": peer}, device_id_type=pl.DeviceIdType.MESH,
        )

    def copy_w(k):
        return pltpu.make_async_copy(w_ref.at[:, at(k)], wbuf.at[k], w_sem.at[k])

    def copy_a(k):
        return remote(part.at[k, 1 - core], got_a.at[k], a_send.at[k], a_recv.at[k], core_peer)

    def copy_b(k):
        return remote(part.at[k, core, 1 - y], got_b.at[k], b_send.at[k], b_recv.at[k], y_peer)

    def copy_c(k, step):
        return remote(
            part.at[k, core, y, z_other(step)], got_c.at[k, z],
            c_send.at[k, z_other(step)], c_recv.at[k, z], z_peer(step),
        )

    def arrive_c(k, step):
        there = z_other(step)
        return remote(
            part.at[k, core, y, there], got_c.at[k, there],
            c_send.at[k, there], c_recv.at[k, there], z_peer(step),
        )

    def copy_own(k):
        return pltpu.make_async_copy(own.at[k], g_ref.at[z, y, core, :, at(k)], own_sem.at[k])

    def copy_z(k, step):
        return remote(
            own.at[k], g_ref.at[z, y, core, :, at(k)],
            z_send.at[k, z_other(step)], z_recv.at[k, z], z_peer(step),
        )

    def arrive_z(k, step):
        there = z_other(step)
        return remote(
            own.at[k], g_ref.at[there, y, core, :, at(k)],
            z_send.at[k, there], z_recv.at[k, there], z_peer(step),
        )

    def copy_y(k):
        here = g_ref.at[:, y, core, :, at(k)]
        return remote(here, here, y_send.at[k], y_recv.at[k], y_peer)

    def arrive_y(k):
        here = g_ref.at[:, 1 - y, core, :, at(k)]
        return remote(here, here, y_send.at[k], y_recv.at[k], y_peer)

    def copy_d(k):
        here = g_ref.at[:, :, core, :, at(k)]
        return remote(here, here, d_send.at[k], d_recv.at[k], core_peer)

    def arrive_d(k):
        here = g_ref.at[:, :, 1 - core, :, at(k)]
        return remote(here, here, d_send.at[k], d_recv.at[k], core_peer)

    @pl.loop(0, chunks)
    def _(k):
        copy_w(k).start()

    barrier = pltpu.get_barrier_semaphore()
    peers = [core_peer, y_peer] + [z_peer(step) for step in range(1, z_count)]
    for peer in peers:
        pl.semaphore_signal(
            barrier, inc=1, device_id={"tp": peer}, device_id_type=pl.DeviceIdType.MESH
        )
    pl.semaphore_wait(barrier, len(peers))

    f32 = jnp.float32

    def stage_a(k):
        copy_w(k).wait()
        value = jnp.dot(att_ref[...], wbuf[k], preferred_element_type=f32)
        part[k] = value.astype(jnp.bfloat16).reshape(part.shape[1:])
        copy_a(k).start()

    def stage_b(k):
        copy_a(k).wait_recv()
        for side in range(2):
            part[k, core, side] = (
                part[k, core, side].astype(f32) + got_a[k, side].astype(f32)
            ).astype(jnp.bfloat16)
        copy_b(k).start()

    def stage_c(k):
        copy_b(k).wait_recv()
        part[k, core, y] = (part[k, core, y].astype(f32) + got_b[k].astype(f32)).astype(
            jnp.bfloat16
        )
        for step in range(1, z_count):
            copy_c(k, step).start()

    def stage_z(k):
        total = part[k, core, y, z].astype(f32)
        for step in range(1, z_count):
            arrive_c(k, step).wait_recv()
            total = total + got_c[k, z_other(step)].astype(f32)
        total = total * sign_ref[k]
        blocks = cols // HB
        tall = jnp.concatenate([total[:, i * HB : (i + 1) * HB] for i in range(blocks)], axis=0)
        tall = jnp.dot(
            tall, had_ref[...], precision=lax.Precision.HIGHEST, preferred_element_type=f32
        )
        turned = jnp.concatenate(
            [tall[i * rows : (i + 1) * rows] for i in range(blocks)], axis=1
        )
        own[k] = (res_ref[:, at(k)].astype(f32) + turned).astype(jnp.bfloat16)
        for step in range(1, z_count):
            copy_z(k, step).start()
        copy_own(k).start()

    def stage_y(k):
        copy_own(k).wait()
        for step in range(1, z_count):
            arrive_z(k, step).wait_recv()
        copy_y(k).start()

    def stage_d(k):
        arrive_y(k).wait_recv()
        copy_d(k).start()

    stages = [stage_a, stage_b, stage_c, stage_z, stage_y, stage_d]

    @pl.loop(0, chunks + len(stages) - 1)
    def _(t):
        for lag, stage in enumerate(stages):
            k = t - lag

            @pl.when((k >= 0) & (k < chunks))
            def _():
                stage(k)

    @pl.loop(0, chunks)
    def _(k):
        arrive_d(k).wait_recv()
        copy_a(k).wait_send()
        copy_b(k).wait_send()
        for step in range(1, z_count):
            copy_c(k, step).wait_send()
            copy_z(k, step).wait_send()
        copy_y(k).wait_send()
        copy_d(k).wait_send()


def norm_kernel(scalars, x_ref, stream_ref, normed_ref):
    x = x_ref[...]

    @pl.when(pl.program_id(0) == scalars[0])
    def _():
        stream_ref[...] = x

    wide = x.astype(jnp.float32)
    mean = jnp.mean(wide * wide, axis=-1, keepdims=True)
    normed_ref[...] = (wide * lax.rsqrt(mean + 1e-05)).astype(jnp.bfloat16)


def body(n, queries, kv_cache, span_kv, prefix_len, residual, out_weight, sign_bits):
    me = lax.axis_index("tp")
    seqs, span, local_cols = queries.shape
    prefix_cap = kv_cache.shape[2]
    width = out_weight.shape[1]
    rows = residual.shape[0]
    z_count = n // 4
    kv_head = me * (local_cols // HD) // (H // KVH)
    bf16 = jnp.bfloat16

    attended = pl.pallas_call(
        attention_kernel,
        grid_spec=pltpu.PrefetchScalarGridSpec(
            num_scalar_prefetch=1,
            grid=(seqs,),
            in_specs=[
                pl.BlockSpec((1, span, local_cols), lambda b, s: (b, 0, 0)),
                pl.BlockSpec((2, 1, prefix_cap, HD), lambda b, s: (0, b, 0, s[0])),
                pl.BlockSpec((2, 1, span, HD), lambda b, s: (0, b, 0, s[0])),
            ],
            out_specs=pl.BlockSpec(
                (2, 2, z_count // seqs, rows, local_cols), lambda b, s: (0, 0, b, 0, 0)
            ),
        ),
        out_shape=jax.ShapeDtypeStruct((2, 2, z_count, rows, local_cols), bf16),
        compiler_params=pltpu.CompilerParams(vmem_limit_bytes=40 * MIB),
    )(
        jnp.concatenate([kv_head[None].astype(jnp.int32), prefix_len]),
        queries, kv_cache, span_kv,
    )

    chunks = width // CHUNK
    signs = (2 * sign_bits - 1).astype(jnp.float32).reshape(chunks, 1, CHUNK)
    vmem = pl.BlockSpec(memory_space=pltpu.VMEM)
    hbm = pl.BlockSpec(memory_space=pl.ANY)
    one = pltpu.SemaphoreType.DMA((chunks,))
    per_z = pltpu.SemaphoreType.DMA((chunks, z_count))
    gathered = pl.pallas_call(
        exchange_kernel,
        out_shape=jax.ShapeDtypeStruct((z_count, 2, 2, rows, width), bf16),
        in_specs=[vmem, hbm, vmem, vmem, vmem],
        out_specs=hbm,
        scratch_shapes=[
            pltpu.VMEM((chunks, local_cols, CHUNK), bf16),
            pltpu.VMEM((chunks, 2, 2, z_count, rows, CHUNK), bf16),
            pltpu.VMEM((chunks, 2, z_count, rows, CHUNK), bf16),
            pltpu.VMEM((chunks, z_count, rows, CHUNK), bf16),
            pltpu.VMEM((chunks, z_count, rows, CHUNK), bf16),
            pltpu.VMEM((chunks, rows, CHUNK), bf16),
            one, one, one, one, one, one, per_z, per_z, per_z, per_z, one, one, one, one,
        ],
        compiler_params=pltpu.CompilerParams(
            collective_id=0, has_side_effects=True, vmem_limit_bytes=56 * MIB
        ),
    )(
        attended.reshape(n * rows, local_cols), out_weight, residual, signs, hadamard(HB),
    )
    gathered = gathered.reshape(n * rows, width)

    stream, normed = pl.pallas_call(
        norm_kernel,
        grid_spec=pltpu.PrefetchScalarGridSpec(
            num_scalar_prefetch=1,
            grid=(n,),
            in_specs=[pl.BlockSpec((rows, width), lambda i, s: (i, 0))],
            out_specs=[
                pl.BlockSpec((rows, width), lambda i, s: (0, 0)),
                pl.BlockSpec((rows, width), lambda i, s: (i, 0)),
            ],
        ),
        out_shape=[
            jax.ShapeDtypeStruct((rows, width), bf16),
            jax.ShapeDtypeStruct((n * rows, width), bf16),
        ],
        compiler_params=pltpu.CompilerParams(vmem_limit_bytes=40 * MIB),
    )(me[None].astype(jnp.int32), gathered)
    return (stream, normed)


def solution(mesh):
    in_specs = (
        P("grp", None, "tp"),
        P(None, "grp", None, None),
        P(None, "grp", None, None),
        P("grp"),
        P(("grp", "tp"), None),
        P("tp", None),
        P(),
    )
    out_specs = (P(("grp", "tp"), None), P("grp", None))
    return jax.shard_map(
        functools.partial(body, mesh.shape["tp"]),
        mesh=mesh, in_specs=in_specs, out_specs=out_specs, check_vma=False,
    )
```

time: 458 us -> 144 us (0.31)
  waiting for transfers between devices: 257 us -> 0 us
  Pallas kernels: 0 us -> 131 us
  local copies, waits for them, and re-layouts: 92 us -> 9.44 us
  other arithmetic: 62.9 us -> 3.25 us
  matrix products: 22.2 us -> 0 us
  between operations: 14.2 us -> 0.68 us
  starting transfers between devices: 7.8 us -> 0 us
    all_to_all x1 -> x0, waiting for transfers between devices: 150 us -> none  [body(): lax.all_to_all(partial_value[None], 'tp', split_axis=1, concat_axis=0, ti...]
    pallas_call x0 -> x3, Pallas kernels: none -> 131 us  [the longest x1 115 us: body(): pl.pallas_call(exchange_kernel, out_shape=jax.ShapeDtypeStruct((z_count,...]
    all_gather x1 -> x0, waiting for transfers between devices: 107 us -> none  [body(): gathered = lax.all_gather(normed, 'tp', axis=0, tiled=True)]
    unnamed x1 -> x0, other arithmetic: 51.2 us -> none
    unnamed x17 -> x10, local copies, waits for them, and re-layouts: 58.2 us -> 9.44 us
    broadcast_in_dim x1 -> x0, local copies, waits for them, and re-layouts: 30.9 us -> none  [body(): partial_value[None]]
    dot_general x3 -> x0, matrix products: 16.3 us -> none  [the longest x1 10.5 us: body(): jnp.dot(attended, out_weight, preferred_element_type=jnp.float32)]
    all_to_all x1 -> x0, starting transfers between devices: 7.58 us -> none  [body(): lax.all_to_all(partial_value[None], 'tp', split_axis=1, concat_axis=0, ti...]
  transfers between devices with their start and end apart: 2 -> 0, of which waited for: 2 -> 0; matrix products, arithmetic and copies ran while one was open for 0% -> 0% of each run, Pallas kernels for 0% -> 0%
where the time goes in v1:
time: 144 us
  Pallas kernels  131 us (91%)
  local copies, waits for them, and re-layouts  9.44 us (7%)
  other arithmetic  3.25 us (2%)
    pallas_call x1, Pallas kernels, body(): pl.pallas_call(exchange_kernel, out_shape=jax.ShapeDtypeStruct((z_count,...  115 us
    pallas_call x1, Pallas kernels, body(): pl.pallas_call(norm_kernel, grid_spec=pltpu.PrefetchScalarGridSpec(num_sc...  9.5 us
    unnamed x10, local copies, waits for them, and re-layouts  9.44 us
    pallas_call x1, Pallas kernels, body(): pl.pallas_call(attention_kernel, grid_spec=pltpu.PrefetchScalarGridSpec(n...  5.88 us

profile of v1, /device:TPU:0, one launch (start us, length us, event | category | flops | bytes accessed | tf_op | source)
XLA Modules:
  0.0 144.1 jit_solution(14455840180789138632)
XLA Ops:
  0.6 0.7 pad_add_fusion.scalars
  1.4 1.5 %add_convert_fusion = f32[16384]{0:T(1024)} fusion(s32[16384]{0:T(1024)} %param.13), kind=kLoop, calls=%fused_computation.8 | loop fusion | flops 49152 | bytes 131072 | tf_op jit(solution)/shard_map/convert_element_type | solution.py:277
  2.9 0.0 copy-start.1
  2.9 3.4 %copy-done.1 = bf16[2,2,2048,512]{3,2,1,0:T(8,128)(2,1)S(1)} copy-done((bf16[2,2,2048,512]{3,2,1,0:T(8,128)(2,1)S(1)}, bf16[2,2,2048,512]{3,2,1,0:T(8,128)(2,1)}, u32[]{:S(2)}) %copy-start.1) | copy-done | bytes 8388632
  6.2 0.0 copy-start.3
  6.2 1.0 copy-done.3
  7.3 0.0 copy-start.4
  7.3 0.9 copy-done.4
  8.2 5.9 %shard_map.86 = bf16[2,2,4,16,512]{4,3,2,1,0:T(8,128)(2,1)S(1)} custom-call(s32[3]{0:T(128)S(1)} %pad_add_fusion.scalars, bf16[2,128,512]{2,1,0:T(8,128)(2,1)S(1)} %copy-done.4, bf16[2,2,2048,512]{3,2,1,0:T(8,128)(2,1)S(1)} %copy-done.1, bf16[2,2,128,512]{3,2,1,0:T(8,128)(2,1)S(1)} %copy-done.3), custom_call_target="tpu_custom_call" | custom-call | tf_op jit(solution)/shard_map/pallas_call | solution.py:255
  14.1 0.0 copy-start.2
  14.1 0.7 copy-done.2
  14.8 1.0 fusion.4.had_ref
  15.9 115.4 %shard_map.87 = bf16[4,2,2,16,16384]{4,3,2,1,0:T(8,128)(2,1)} custom-call(bf16[256,512]{1,0:T(8,128)(2,1)} %bitcast.6, bf16[512,16384]{1,0:T(8,128)(2,1)} %w_ref.1, bf16[16,16384]{1,0:T(8,128)(2,1)} %res_ref.1, f32[16,1,1024]{2,1,0:T(1,128)} %bitcast.7, f32[256,256]{1,0:T(8,128)} %fusion.4.had_ref), custom_call_target="tpu_custom_call" | custom-call | tf_op jit(solution)/shard_map/pallas_call | solution.py:282
  131.2 0.0 copy-start
  131.3 3.4 %copy-done = bf16[4,2,2,16,16384]{4,3,2,1,0:T(8,128)(2,1)S(1)} copy-done((bf16[4,2,2,16,16384]{4,3,2,1,0:T(8,128)(2,1)S(1)}, bf16[4,2,2,16,16384]{4,3,2,1,0:T(8,128)(2,1)}, u32[]{:S(2)}) %copy-start) | copy-done | bytes 8388632
  134.6 9.5 %shard_map.88 = (bf16[16,16384]{1,0:T(8,128)(2,1)}, bf16[256,16384]{1,0:T(8,128)(2,1)}) custom-call(s32[1]{0:T(128)} %bitcast.scalars, bf16[256,16384]{1,0:T(8,128)(2,1)S(1)} %bitcast.5), custom_call_target="tpu_custom_call" | custom-call | tf_op jit(solution)/shard_map/pallas_call | solution.py:304
Async XLA Ops:
  2.9 3.4 %copy-start.1 = (bf16[2,2,2048,512]{3,2,1,0:T(8,128)(2,1)S(1)}, bf16[2,2,2048,512]{3,2,1,0:T(8,128)(2,1)}, u32[]{:S(2)}) copy-start(bf16[2,2,2048,512]{3,2,1,0:T(8,128)(2,1)} %cache_ref.1) | copy-start | bytes 25165828
  6.2 1.0 copy-start.3
  7.3 0.9 copy-start.4
  14.1 0.7 copy-start.2
  131.2 3.4 %copy-start = (bf16[4,2,2,16,16384]{4,3,2,1,0:T(8,128)(2,1)S(1)}, bf16[4,2,2,16,16384]{4,3,2,1,0:T(8,128)(2,1)}, u32[]{:S(2)}) copy-start(bf16[4,2,2,16,16384]{4,3,2,1,0:T(8,128)(2,1)} %shard_map.87) | copy-start | bytes 25165828

commit v2 on v1

v2 whole, which is shorter than its diff:
```python
import functools
import math

import jax
import jax.numpy as jnp
from jax import lax
from jax.experimental import pallas as pl
from jax.experimental.pallas import tpu as pltpu
from jax.sharding import PartitionSpec as P

H = 64
KVH = 4
HD = 128
HB = 256
CHUNK = 1024
NORM_ROWS = 128
LAGS = (0, 2, 4, 6, 8, 10, 12, 14)
LAGS = (0, 2, 4, 6, 8, 10, 12, 14)
MIB = 1 << 20


def hadamard(size):
    common = lax.broadcasted_iota(jnp.int32, (size, size), 0)
    common = common & lax.broadcasted_iota(jnp.int32, (size, size), 1)
    for shift in (16, 8, 4, 2, 1):
        common = common ^ (common >> shift)
    return (1 - 2 * (common & 1)).astype(jnp.float32) / math.sqrt(size)


def attention_kernel(kv_head, lengths, q_ref, cache_ref, span_ref, out_ref):
    seq = pl.program_id(0)
    length = lengths[seq]
    prefix_cap = cache_ref.shape[2]
    span = span_ref.shape[2]
    _, _, z_here, rows, local_cols = out_ref.shape
    scale = math.log2(math.e) / math.sqrt(HD)
    keys, values = cache_ref[0, 0], cache_ref[1, 0]
    span_keys, span_values = span_ref[0, 0], span_ref[1, 0]
    trans = (((1,), (1,)), ((), ()))
    shown = lax.broadcasted_iota(jnp.int32, (span, prefix_cap), 1) < length
    token = lax.broadcasted_iota(jnp.int32, (span, span), 0)
    causal = lax.broadcasted_iota(jnp.int32, (span, span), 1) <= token
    for head in range(local_cols // HD):
        at = slice(head * HD, (head + 1) * HD)
        q = q_ref[0, :, at]
        s0 = lax.dot_general(q, keys, trans, preferred_element_type=jnp.float32)
        s1 = lax.dot_general(q, span_keys, trans, preferred_element_type=jnp.float32)
        s0 = jnp.where(shown, s0, -1e30)
        s1 = jnp.where(causal, s1, -1e30)
        top = jnp.maximum(jnp.max(s0, axis=1, keepdims=True), jnp.max(s1, axis=1, keepdims=True))
        p0 = jnp.exp2((s0 - top) * scale)
        p1 = jnp.exp2((s1 - top) * scale)
        total = jnp.sum(p0, axis=1, keepdims=True) + jnp.sum(p1, axis=1, keepdims=True)
        mixed = jnp.dot(p0.astype(jnp.bfloat16), values, preferred_element_type=jnp.float32)
        mixed += jnp.dot(p1.astype(jnp.bfloat16), span_values, preferred_element_type=jnp.float32)
        mixed = (mixed / total).astype(jnp.bfloat16)
        for z in range(z_here):
            for y in range(2):
                for core in range(2):
                    first = ((z * 2 + y) * 2 + core) * rows
                    out_ref[core, y, z, :, at] = mixed[first : first + rows]


def exchange_kernel(
    att_ref, w_ref, res_ref, sign_ref, g_ref,
    wbuf, part, got_a, got_b, got_bz, got_c, got_d, own, had_ref,
    w_sem, own_sem, a_send, a_recv, b_send, b_recv, c_send, c_recv, d_send, d_recv,
    e_send, e_recv, f_send, f_recv, g_send, g_recv, h_send, h_recv,
):
    chunks, far_count, rows, cols = got_d.shape
    me = lax.axis_index("tp")
    core = lax.rem(me, 2)
    y = lax.rem(me // 2, 2)
    near = lax.rem(me // 4, 2)
    far = me // 8
    core_peer = me + 1 - 2 * core
    y_peer = me + 2 - 4 * y
    near_peer = me + 4 - 8 * near
    others = range(1, far_count)

    def far_other(step):
        return lax.rem(far + step, far_count)

    def far_peer(step):
        return far_other(step) * 8 + near * 4 + y * 2 + core

    def at(k):
        return pl.ds(pl.multiple_of(k * cols, cols), cols)

    def remote(src, dst, send, recv, peer):
        return pltpu.make_async_remote_copy(
            src_ref=src, dst_ref=dst, send_sem=send, recv_sem=recv,
            device_id={"tp": peer}, device_id_type=pl.DeviceIdType.MESH,
        )

    def by_kind(k, y_first, near_first):
        kind = lax.rem(k, 4)
        pl.when(kind != 1)(y_first)
        pl.when(kind == 1)(near_first)

    def copy_w(k):
        return pltpu.make_async_copy(w_ref.at[:, at(k)], wbuf.at[k], w_sem.at[k])

    def copy_a(k):
        return remote(part.at[k, 1 - core], got_a.at[k], a_send.at[k], a_recv.at[k], core_peer)

    def copy_b_y(k):
        return remote(part.at[k, core, 1 - y], got_b.at[k], b_send.at[k], b_recv.at[k], y_peer)

    def copy_b_near(k):
        return remote(
            part.at[k, core, :, :, 1 - near], got_bz.at[k], b_send.at[k], b_recv.at[k], near_peer
        )

    def copy_c_near(k):
        return remote(
            part.at[k, core, y, :, 1 - near], got_c.at[k], c_send.at[k], c_recv.at[k], near_peer
        )

    def copy_c_y(k):
        return remote(
            part.at[k, core, 1 - y, :, near], got_c.at[k], c_send.at[k], c_recv.at[k], y_peer
        )

    def copy_d(k, step):
        there = far_other(step)
        return remote(
            part.at[k, core, y, there, near], got_d.at[k, far],
            d_send.at[k, there], d_recv.at[k, far], far_peer(step),
        )

    def arrive_d(k, step):
        there = far_other(step)
        return remote(
            part.at[k, core, y, there, near], got_d.at[k, there],
            d_send.at[k, there], d_recv.at[k, there], far_peer(step),
        )

    def copy_own(k):
        return pltpu.make_async_copy(
            own.at[k], g_ref.at[far, near, y, core, :, at(k)], own_sem.at[k]
        )

    def copy_e(k, step):
        return remote(
            own.at[k], g_ref.at[far, near, y, core, :, at(k)],
            e_send.at[k, far_other(step)], e_recv.at[k, far], far_peer(step),
        )

    def arrive_e(k, step):
        there = far_other(step)
        return remote(
            own.at[k], g_ref.at[there, near, y, core, :, at(k)],
            e_send.at[k, there], e_recv.at[k, there], far_peer(step),
        )

    def copy_f(k, near_at, y_at, peer):
        here = g_ref.at[:, near_at, y_at, core, :, at(k)]
        return remote(here, here, f_send.at[k], f_recv.at[k], peer)

    def copy_g_y(k, y_at):
        here = g_ref.at[:, :, y_at, core, :, at(k)]
        return remote(here, here, g_send.at[k], g_recv.at[k], y_peer)

    def copy_g_near(k, near_at):
        here = g_ref.at[:, near_at, :, core, :, at(k)]
        return remote(here, here, g_send.at[k], g_recv.at[k], near_peer)

    def copy_h(k, core_at):
        here = g_ref.at[:, :, :, core_at, :, at(k)]
        return remote(here, here, h_send.at[k], h_recv.at[k], core_peer)

    @pl.loop(0, chunks)
    def _(k):
        copy_w(k).start()

    barrier = pltpu.get_barrier_semaphore()
    peers = [core_peer, y_peer, near_peer] + [far_peer(step) for step in others]
    for peer in peers:
        pl.semaphore_signal(
            barrier, inc=1, device_id={"tp": peer}, device_id_type=pl.DeviceIdType.MESH
        )
    had_ref[...] = hadamard(HB)
    pl.semaphore_wait(barrier, len(peers))

    f32 = jnp.float32

    def plus(left, right):
        return (left.astype(f32) + right.astype(f32)).astype(jnp.bfloat16)

    def stage_a(k):
        copy_w(k).wait()
        value = jnp.dot(att_ref[...], wbuf[k], preferred_element_type=f32)
        part[k] = value.astype(jnp.bfloat16).reshape(part.shape[1:])
        copy_a(k).start()

    def stage_b(k):
        copy_a(k).wait_recv()
        for side in range(2):
            part[k, core, side] = plus(part[k, core, side], got_a[k, side])
        by_kind(k, lambda: copy_b_y(k).start(), lambda: copy_b_near(k).start())

    def stage_c(k):
        def y_first():
            copy_b_y(k).wait_recv()
            part[k, core, y] = plus(part[k, core, y], got_b[k])
            copy_c_near(k).start()

        def near_first():
            copy_b_near(k).wait_recv()
            for side in range(2):
                for block in range(far_count):
                    part[k, core, side, block, near] = plus(
                        part[k, core, side, block, near], got_bz[k, side, block]
                    )
            copy_c_y(k).start()

        by_kind(k, y_first, near_first)

    def stage_d(k):
        by_kind(k, lambda: copy_c_near(k).wait_recv(), lambda: copy_c_y(k).wait_recv())
        for block in range(far_count):
            part[k, core, y, block, near] = plus(
                part[k, core, y, block, near], got_c[k, block]
            )
        for step in others:
            copy_d(k, step).start()

    def stage_e(k):
        total = part[k, core, y, far, near].astype(f32)
        for step in others:
            arrive_d(k, step).wait_recv()
            total = total + got_d[k, far_other(step)].astype(f32)
        total = total * (2 * sign_ref[:, at(k)] - 1).astype(f32)
        blocks = cols // HB
        tall = jnp.concatenate([total[:, i * HB : (i + 1) * HB] for i in range(blocks)], axis=0)
        tall = jnp.dot(
            tall, had_ref[...], precision=lax.Precision.HIGHEST, preferred_element_type=f32
        )
        turned = jnp.concatenate(
            [tall[i * rows : (i + 1) * rows] for i in range(blocks)], axis=1
        )
        own[k] = (res_ref[:, at(k)].astype(f32) + turned).astype(jnp.bfloat16)
        for step in others:
            copy_e(k, step).start()
        copy_own(k).start()

    def stage_f(k):
        copy_own(k).wait()
        for step in others:
            arrive_e(k, step).wait_recv()
        by_kind(
            k,
            lambda: copy_f(k, near, y, near_peer).start(),
            lambda: copy_f(k, near, y, y_peer).start(),
        )

    def stage_g(k):
        def y_last():
            copy_f(k, 1 - near, y, near_peer).wait_recv()
            copy_g_y(k, y).start()

        def near_last():
            copy_f(k, near, 1 - y, y_peer).wait_recv()
            copy_g_near(k, near).start()

        by_kind(k, y_last, near_last)

    def stage_h(k):
        by_kind(
            k,
            lambda: copy_g_y(k, 1 - y).wait_recv(),
            lambda: copy_g_near(k, 1 - near).wait_recv(),
        )
        copy_h(k, core).start()

    stages = [stage_a, stage_b, stage_c, stage_d, stage_e, stage_f, stage_g, stage_h]

    @pl.loop(0, chunks + LAGS[-1])
    def _(t):
        for lag, stage in zip(LAGS, stages):
            k = t - lag

            @pl.when((k >= 0) & (k < chunks))
            def _():
                stage(k)

    @pl.loop(0, chunks)
    def _(k):
        copy_h(k, 1 - core).wait_recv()
        copy_a(k).wait_send()

        def y_kind():
            copy_b_y(k).wait_send()
            copy_c_near(k).wait_send()
            copy_f(k, near, y, near_peer).wait_send()
            copy_g_y(k, y).wait_send()

        def near_kind():
            copy_b_near(k).wait_send()
            copy_c_y(k).wait_send()
            copy_f(k, near, y, y_peer).wait_send()
            copy_g_near(k, near).wait_send()

        by_kind(k, y_kind, near_kind)
        for step in others:
            copy_d(k, step).wait_send()
            copy_e(k, step).wait_send()
        copy_h(k, core).wait_send()


def norm_kernel(scalars, x_ref, stream_ref, normed_ref):
    rows, width = stream_ref.shape
    groups = x_ref.shape[0] // rows
    for group in range(groups):
        here = slice(group * rows, (group + 1) * rows)

        @pl.when(pl.program_id(0) * groups + group == scalars[0])
        def _():
            stream_ref[...] = x_ref[here]

        pieces = [slice(first, first + 1024) for first in range(0, width, 1024)]
        squares = jnp.zeros((rows, 1024), jnp.float32)
        for piece in pieces:
            wide = x_ref[here, piece].astype(jnp.float32)
            squares = squares + wide * wide
        mean = jnp.sum(squares, axis=-1, keepdims=True) / width
        factor = lax.rsqrt(mean + 1e-05)
        for piece in pieces:
            wide = x_ref[here, piece].astype(jnp.float32)
            normed_ref[here, piece] = (wide * factor).astype(jnp.bfloat16)


def body(n, queries, kv_cache, span_kv, prefix_len, residual, out_weight, sign_bits):
    me = lax.axis_index("tp")
    seqs, span, local_cols = queries.shape
    prefix_cap = kv_cache.shape[2]
    width = out_weight.shape[1]
    rows = residual.shape[0]
    z_count, far_count = n // 4, n // 8
    kv_head = me * (local_cols // HD) // (H // KVH)
    bf16 = jnp.bfloat16

    attended = pl.pallas_call(
        attention_kernel,
        grid_spec=pltpu.PrefetchScalarGridSpec(
            num_scalar_prefetch=2,
            grid=(seqs,),
            in_specs=[
                pl.BlockSpec((1, span, local_cols), lambda b, s, _: (b, 0, 0)),
                pl.BlockSpec((2, 1, prefix_cap, HD), lambda b, s, _: (0, b, 0, s[0])),
                pl.BlockSpec((2, 1, span, HD), lambda b, s, _: (0, b, 0, s[0])),
            ],
            out_specs=pl.BlockSpec(
                (2, 2, z_count // seqs, rows, local_cols), lambda b, s, _: (0, 0, b, 0, 0)
            ),
        ),
        out_shape=jax.ShapeDtypeStruct((2, 2, z_count, rows, local_cols), bf16),
        compiler_params=pltpu.CompilerParams(vmem_limit_bytes=60 * MIB),
    )(
        kv_head[None].astype(jnp.int32), prefix_len,
        queries, kv_cache, span_kv,
    )

    chunks = width // CHUNK
    vmem = pl.BlockSpec(memory_space=pltpu.VMEM)
    hbm = pl.BlockSpec(memory_space=pl.ANY)
    one = pltpu.SemaphoreType.DMA((chunks,))
    per_far = pltpu.SemaphoreType.DMA((chunks, far_count))
    gathered = pl.pallas_call(
        exchange_kernel,
        out_shape=jax.ShapeDtypeStruct((far_count, 2, 2, 2, rows, width), bf16),
        in_specs=[vmem, hbm, vmem, vmem],
        out_specs=hbm,
        scratch_shapes=[
            pltpu.VMEM((chunks, local_cols, CHUNK), bf16),
            pltpu.VMEM((chunks, 2, 2, far_count, 2, rows, CHUNK), bf16),
            pltpu.VMEM((chunks, 2, far_count, 2, rows, CHUNK), bf16),
            pltpu.VMEM((chunks, far_count, 2, rows, CHUNK), bf16),
            pltpu.VMEM((chunks, 2, far_count, rows, CHUNK), bf16),
            pltpu.VMEM((chunks, far_count, rows, CHUNK), bf16),
            pltpu.VMEM((chunks, far_count, rows, CHUNK), bf16),
            pltpu.VMEM((chunks, rows, CHUNK), bf16),
            pltpu.VMEM((HB, HB), jnp.float32),
            one, one, one, one, one, one, one, one, per_far, per_far,
            per_far, per_far, one, one, one, one, one, one,
        ],
        compiler_params=pltpu.CompilerParams(
            collective_id=0, has_side_effects=True, vmem_limit_bytes=56 * MIB
        ),
    )(
        attended.reshape(n * rows, local_cols), out_weight, residual, sign_bits[None],
    )
    gathered = gathered.reshape(n * rows, width)

    stream, normed = pl.pallas_call(
        norm_kernel,
        grid_spec=pltpu.PrefetchScalarGridSpec(
            num_scalar_prefetch=1,
            grid=(n * rows // NORM_ROWS,),
            in_specs=[pl.BlockSpec((NORM_ROWS, width), lambda i, s: (i, 0))],
            out_specs=[
                pl.BlockSpec((rows, width), lambda i, s: (0, 0)),
                pl.BlockSpec((NORM_ROWS, width), lambda i, s: (i, 0)),
            ],
        ),
        out_shape=[
            jax.ShapeDtypeStruct((rows, width), bf16),
            jax.ShapeDtypeStruct((n * rows, width), bf16),
        ],
        compiler_params=pltpu.CompilerParams(vmem_limit_bytes=60 * MIB),
    )(me[None].astype(jnp.int32), gathered)
    return (stream, normed)


def solution(mesh):
    in_specs = (
        P("grp", None, "tp"),
        P(None, "grp", None, None),
        P(None, "grp", None, None),
        P("grp"),
        P(("grp", "tp"), None),
        P("tp", None),
        P(),
    )
    out_specs = (P(("grp", "tp"), None), P("grp", None))
    return jax.shard_map(
        functools.partial(body, mesh.shape["tp"]),
        mesh=mesh, in_specs=in_specs, out_specs=out_specs, check_vma=False,
    )
```

time: 144 us -> 118 us (0.82)
  Pallas kernels: 131 us -> 117 us
  local copies, waits for them, and re-layouts: 9.44 us -> 0 us
  other arithmetic: 3.25 us -> 0 us
    pallas_call x1, Pallas kernels: 115 us -> 102 us  [body(): pl.pallas_call(exchange_kernel, out_shape=jax.ShapeDtypeStruct((far_count...]
    unnamed x10 -> x0, local copies, waits for them, and re-layouts: 9.44 us -> none
    pallas_call x1, Pallas kernels: 5.88 us -> 7.55 us  [body(): pl.pallas_call(attention_kernel, grid_spec=pltpu.PrefetchScalarGridSpec(n...]
    pallas_call x1, Pallas kernels: 9.5 us -> 7.89 us  [body(): pl.pallas_call(norm_kernel, grid_spec=pltpu.PrefetchScalarGridSpec(num_sc...]
    convert_element_type x1 -> x0, other arithmetic: 1.48 us -> none  [body(): signs = (2 * sign_bits - 1).astype(jnp.float32).reshape(chunks, 1, CHUNK)]
where the time goes in v2:
time: 118 us
  Pallas kernels  117 us (99%)
    pallas_call x1, Pallas kernels, body(): pl.pallas_call(exchange_kernel, out_shape=jax.ShapeDtypeStruct((far_count...  102 us
    pallas_call x1, Pallas kernels, body(): pl.pallas_call(norm_kernel, grid_spec=pltpu.PrefetchScalarGridSpec(num_sc...  7.89 us
    pallas_call x1, Pallas kernels, body(): pl.pallas_call(attention_kernel, grid_spec=pltpu.PrefetchScalarGridSpec(n...  7.55 us

profile of v2, /device:TPU:0, one launch (start us, length us, event | category | flops | bytes accessed | tf_op | source)
XLA Modules:
  0.0 117.7 jit_solution(4731272945962740395)
XLA Ops:
  0.6 7.6 %shard_map.86 = bf16[2,2,4,16,512]{4,3,2,1,0:T(8,128)(2,1)} custom-call(s32[1]{0:T(128)} %bitcast.1.kv_head, s32[2]{0:T(128)} %lengths.1, bf16[2,128,512]{2,1,0:T(8,128)(2,1)} %q_ref.1, bf16[2,2,2048,512]{3,2,1,0:T(8,128)(2,1)} %cache_ref.1, bf16[2,2,128,512]{3,2,1,0:T(8,128)(2,1)} %span_ref.1), custom_call_target="tpu_custom_call" | custom-call | tf_op jit(solution)/shard_map/pallas_call | solution.py:344
  8.2 101.6 %shard_map.87 = bf16[2,2,2,2,16,16384]{5,4,3,2,1,0:T(8,128)(2,1)} custom-call(bf16[256,512]{1,0:T(8,128)(2,1)} %bitcast.6, bf16[512,16384]{1,0:T(8,128)(2,1)} %w_ref.1, bf16[16,16384]{1,0:T(8,128)(2,1)} %res_ref.1, s32[1,16384]{1,0:T(1,128)} %bitcast.7), custom_call_target="tpu_custom_call" | custom-call | tf_op jit(solution)/shard_map/pallas_call | solution.py:370
  109.8 7.9 %shard_map.88 = (bf16[16,16384]{1,0:T(8,128)(2,1)}, bf16[256,16384]{1,0:T(8,128)(2,1)}) custom-call(s32[1]{0:T(128)} %bitcast.scalars, bf16[256,16384]{1,0:T(8,128)(2,1)} %bitcast.5), custom_call_target="tpu_custom_call" | custom-call | tf_op jit(solution)/shard_map/pallas_call | solution.py:396

commit v3 on v2

--- a/solution.py
+++ b/solution.py
@@ -14,7 +14,6 @@
 HB = 256
 CHUNK = 1024
 NORM_ROWS = 128
-LAGS = (0, 2, 4, 6, 8, 10, 12, 14)
 LAGS = (0, 2, 4, 6, 8, 10, 12, 14)
 MIB = 1 << 20
 
@@ -94,7 +93,7 @@
         )
 
     def by_kind(k, y_first, near_first):
-        kind = lax.rem(k, 4)
+        kind = lax.rem(k, 3)
         pl.when(kind != 1)(y_first)
         pl.when(kind == 1)(near_first)
 

time: 118 us -> 118 us (level)
  no operation moved by 1% of the time
where the time goes in v3:
time: 118 us
  Pallas kernels  117 us (99%)
    pallas_call x1, Pallas kernels, body(): pl.pallas_call(exchange_kernel, out_shape=jax.ShapeDtypeStruct((far_count...  102 us
    pallas_call x1, Pallas kernels, body(): pl.pallas_call(norm_kernel, grid_spec=pltpu.PrefetchScalarGridSpec(num_sc...  7.89 us
    pallas_call x1, Pallas kernels, body(): pl.pallas_call(attention_kernel, grid_spec=pltpu.PrefetchScalarGridSpec(n...  7.55 us

profile of v3, /device:TPU:0, one launch (start us, length us, event | category | flops | bytes accessed | tf_op | source)
XLA Modules:
  0.0 117.6 jit_solution(16832800843497328477)
XLA Ops:
  0.6 7.6 %shard_map.86 = bf16[2,2,4,16,512]{4,3,2,1,0:T(8,128)(2,1)} custom-call(s32[1]{0:T(128)} %bitcast.1.kv_head, s32[2]{0:T(128)} %lengths.1, bf16[2,128,512]{2,1,0:T(8,128)(2,1)} %q_ref.1, bf16[2,2,2048,512]{3,2,1,0:T(8,128)(2,1)} %cache_ref.1, bf16[2,2,128,512]{3,2,1,0:T(8,128)(2,1)} %span_ref.1), custom_call_target="tpu_custom_call" | custom-call | tf_op jit(solution)/shard_map/pallas_call | solution.py:343
  8.2 101.5 %shard_map.87 = bf16[2,2,2,2,16,16384]{5,4,3,2,1,0:T(8,128)(2,1)} custom-call(bf16[256,512]{1,0:T(8,128)(2,1)} %bitcast.6, bf16[512,16384]{1,0:T(8,128)(2,1)} %w_ref.1, bf16[16,16384]{1,0:T(8,128)(2,1)} %res_ref.1, s32[1,16384]{1,0:T(1,128)} %bitcast.7), custom_call_target="tpu_custom_call" | custom-call | tf_op jit(solution)/shard_map/pallas_call | solution.py:369
  109.7 7.9 %shard_map.88 = (bf16[16,16384]{1,0:T(8,128)(2,1)}, bf16[256,16384]{1,0:T(8,128)(2,1)}) custom-call(s32[1]{0:T(128)} %bitcast.scalars, bf16[256,16384]{1,0:T(8,128)(2,1)} %bitcast.5), custom_call_target="tpu_custom_call" | custom-call | tf_op jit(solution)/shard_map/pallas_call | solution.py:395
